TPU v7x, 32 devices: a whole 2x2x4 slice. The times are simulated.
32 devices in a mesh: tile: 8 (over y, x, core), mode: 4 (over z).
Axes of the slice: x: 2, y: 2, z: 4, core: 2. Of those that a mesh axis runs over, the one named last changes fastest.
Arguments:
- mode_shapes: bfloat16 [64, 64, 2048], P('mode', 'tile'), may hold values from -6 to 6
- stiffness: float32 [64, 2048], P('tile'), may hold values from 0.5 to 4
- node_slot: int32 [64, 2048], P('tile'), may hold values from 0 to 63, as said below
- slot_zone: int32 [8, 8, 8], replicated, may hold values from 0 to 63, as said below
Outputs:
- energy: float32 [512, 64, 64], P('tile', 'mode')
Inputs may be any that keep to these rules, and one draw needn't show every extreme that they name: `slot_zone`: for each tile and owner, the 8 zone numbers are distinct. `node_slot`: slots that no node of a tile names carry no zone's nodes.
All inputs are finite; a program needn't handle non-finite values.
Results may differ from a plain program's by a relative error of at most 0.00099.
Values may be sent and summed in bfloat16 or wider, within the bound.
A program may use at most 64 MiB of HBM per device.

v0:
```python
import math

import jax
import jax.numpy as jnp
from jax import lax
from jax.sharding import PartitionSpec as P

ZONES = 512


POISSON = 0.3
SHEAR = 2.0 * (1.0 - POISSON)


def with_halo(cells, sides, width):
    for axis, dim in sides:
        count = lax.axis_size(axis)
        ends = count - 1
        head = lax.slice_in_dim(cells, 0, width, axis=dim)
        tail = lax.slice_in_dim(cells, cells.shape[dim] - width, cells.shape[dim], axis=dim)
        cells = jnp.concatenate(
            [
                lax.ppermute(tail, axis, [(i, (i + 1) % count) for i in range(ends)]),
                cells,
                lax.ppermute(head, axis, [((i + 1) % count, i) for i in range(ends)]),
            ],
            axis=dim,
        )
    return cells


def curvatures(shapes_framed):
    framed = jnp.pad(shapes_framed, ((0, 0), (0, 0), (1, 1)))
    centre = framed[:, 1:-1, 1:-1]
    along_x = framed[:, 2:, 1:-1] - 2.0 * centre + framed[:, :-2, 1:-1]
    along_y = framed[:, 1:-1, 2:] - 2.0 * centre + framed[:, 1:-1, :-2]
    twist_xy = 0.25 * (
        framed[:, 2:, 2:] - framed[:, 2:, :-2] - framed[:, :-2, 2:] + framed[:, :-2, :-2]
    )
    return jnp.stack([along_x, along_y, twist_xy]).astype(jnp.bfloat16)


def left_factor(bending, stiffness):
    along_x, along_y, twist_xy = (bending[0], bending[1], bending[2])
    return jnp.stack(
        [
            stiffness * (along_x + POISSON * along_y),
            stiffness * (along_y + POISSON * along_x),
            stiffness * (SHEAR * twist_xy),
        ]
    )


def per_device(mode_shapes, stiffness, node_slot, slot_zone):
    panel_modes, tile_rows, row_cells = mode_shapes.shape
    node_count = tile_rows * row_cells
    tile_count = lax.axis_size("tile")
    mode_count = panel_modes * lax.axis_size("mode")
    owner_slots = slot_zone.shape[2]
    slot_count = tile_count * owner_slots
    owned_zones = ZONES // tile_count
    pair_count = panel_modes * mode_count
    padded = with_halo(mode_shapes, (("tile", 1),), 1)
    own_bending = curvatures(padded.astype(jnp.float32))
    own_float = own_bending.astype(jnp.float32)
    weighted = left_factor(own_float, stiffness)
    own_sums = jnp.sum(weighted * own_float, axis=(0, 2, 3))
    placed_sums = lax.dynamic_update_slice_in_dim(
        jnp.zeros((mode_count,), jnp.float32), own_sums, lax.axis_index("mode") * panel_modes, 0
    )
    totals = 0.5 * lax.psum(placed_sums, ("tile", "mode"))
    gathered_bend = lax.all_gather(own_bending, "mode", axis=1, tiled=True)
    right_flat = gathered_bend.reshape(3, mode_count, node_count)
    left_flat = weighted.astype(jnp.bfloat16).reshape(3, panel_modes, node_count)
    slot_flat = node_slot.reshape(node_count)
    slot_range = jnp.arange(slot_count, dtype=jnp.int32)
    block_nodes = math.gcd(node_count, max(128, (1 << 20) // pair_count))

    def one_block(number, running):
        first_node = number * block_nodes
        left_block = lax.dynamic_slice_in_dim(left_flat, first_node, block_nodes, 2).astype(
            jnp.float32
        )
        right_block = lax.dynamic_slice_in_dim(right_flat, first_node, block_nodes, 2).astype(
            jnp.float32
        )
        slot_block = lax.dynamic_slice_in_dim(slot_flat, first_node, block_nodes, 0)
        products = jnp.sum(left_block[:, :, None, :] * right_block[:, None, :, :], axis=0)
        products = products.reshape(pair_count, block_nodes)
        member_block = (slot_block[:, None] == slot_range[None, :]).astype(jnp.float32)
        return running + jnp.dot(products, member_block, precision=lax.Precision.HIGHEST)

    by_pair = lax.fori_loop(
        0, node_count // block_nodes, one_block, jnp.zeros((pair_count, slot_count), jnp.float32)
    )
    routed = by_pair.T.reshape(tile_count, owner_slots, pair_count)
    tile_index = lax.axis_index("tile")
    arrived = lax.all_to_all(routed, "tile", split_axis=0, concat_axis=0, tiled=True)
    sources = lax.dynamic_index_in_dim(slot_zone, tile_index, 1, keepdims=False)
    selector = (
        sources.reshape(tile_count * owner_slots)[:, None]
        == jnp.arange(owned_zones, dtype=jnp.int32)[None, :]
    ).astype(jnp.float32)
    summed = jnp.dot(
        selector.T,
        arrived.reshape(tile_count * owner_slots, pair_count),
        precision=lax.Precision.HIGHEST,
    )
    own_totals = lax.dynamic_slice_in_dim(
        totals, lax.axis_index("mode") * panel_modes, panel_modes, 0
    )
    denominator = jnp.sqrt(own_totals[:, None] * totals[None, :])
    return ZONES * (0.5 * summed.reshape(owned_zones, panel_modes, mode_count)) / denominator


def solution(mesh):
    placed = (P("mode", "tile", None), P("tile", None), P("tile", None), P())
    return jax.shard_map(
        per_device, mesh=mesh, in_specs=placed, out_specs=P("tile", "mode", None), check_vma=False
    )
```

profile of v0, /device:TPU:0, one launch (start us, length us, event | category | flops | bytes accessed | tf_op | source)
XLA Modules:
  0.0 321.5 jit_solution(13397393172898404229)
XLA Ops:
  11.6 4.0 %collective-permute-done.1 = bf16[16,1,2048]{2,1,0:T(2,128)(2,1)S(1)} collective-permute-done((bf16[16,1,2048]{2,1,0:T(2,128)(2,1)S(1)}, bf16[16,1,2048]{2,1,0:T(2,128)(2,1)S(1)}, u32[]{:S(2)}, u32[]{:S(2)}) %collective-permute-start.1) | collective-permute-done | bytes 65568 | tf_op jit(solution)/shard_map/ppermute | solution.py:25
  31.3 51.6 %psum.7 = f32[64]{0:T(128)S(1)} all-reduce(f32[64]{0:T(128)S(1)} %dynamic_update_slice.3), channel_id=1, replica_groups=mesh['tile'=8,'mode'=4] {'tile','mode'}, use_global_device_ids=true, to_apply=%region_4.5 | all-reduce | flops 64 | bytes 512 | tf_op jit(solution)/shard_map/psum | solution.py:71
  84.2 57.6 %all-gather.2.cloned.1.call-done = bf16[3,64,8,2048]{3,2,1,0:T(8,128)(2,1)} async-done(((bf16[3,16,8,2048]{3,2,1,0:T(8,128)(2,1)}), bf16[3,64,8,2048]{3,2,1,0:T(8,128)(2,1)}) %all-gather.2.cloned.1.call-update) | async-done | bytes 6291472 | tf_op jit(solution)/shard_map/all_gather | solution.py:72
  141.8 10.5 %reshape.63 = bf16[3,64,16384]{2,1,0:T(8,128)(2,1)} reshape(bf16[3,64,8,2048]{3,2,1,0:T(8,128)(2,1)} %all-gather.2.cloned.1.call-done) | data formatting | bytes 12582912 | tf_op jit(solution)/shard_map/reshape | solution.py:73
  152.3 149.7 %while.14 = (s32[]{:T(128)}, f32[1024,64]{0,1:T(8,128)}, bf16[3,16,16384]{2,1,0:T(8,128)(2,1)S(1)}, bf16[3,64,16384]{2,1,0:T(8,128)(2,1)}, s32[16384]{0:T(1024)S...) while((s32[]{:T(128)}, f32[1024,64]{0,1:T(8,128)}, bf16[3,16,16384]{2,1,0:T(8,128)(2,1)S(1)}, ...), condition=%wide.region_2.3_spmd.clone, body=%wide.region_0.0_spmd.clone.sunk | while | flops 810991616 | bytes 11382945 | solution.py:93
  153.4 3.0 multiply_reduce_fusion.2
  156.4 5.2 %convolution_add_fusion.2 = f32[1024,64]{0,1:T(8,128)} fusion(f32[1024,1024]{1,0:T(8,128)} %bitcast.33, f32[1024,64]{0,1:T(8,128)} %get-tuple-element.203, s32[1024]{0:T(1024)S(1)} %dynamic_slice.41, pred[]{:T(512)S(6)} %compare.4), kind=kOutput, calls=%fused_computation.2.clone.1 | convolution fusion | flops 805502976 | bytes 4722689 | tf_op jit(solution)/shard_map/while/body/eval_jaxpr/dot_general | solution.py:91
  162.7 3.0 multiply_reduce_fusion.2
  165.7 5.2 %convolution_add_fusion.2 = f32[1024,64]{0,1:T(8,128)} fusion(f32[1024,1024]{1,0:T(8,128)} %bitcast.33, f32[1024,64]{0,1:T(8,128)} %get-tuple-element.203, s32[1024]{0:T(1024)S(1)} %dynamic_slice.41, pred[]{:T(512)S(6)} %compare.4), kind=kOutput, calls=%fused_computation.2.clone.1 | convolution fusion | flops 805502976 | bytes 4722689 | tf_op jit(solution)/shard_map/while/body/eval_jaxpr/dot_general | solution.py:91
  172.0 3.0 multiply_reduce_fusion.2
  175.1 5.2 %convolution_add_fusion.2 = f32[1024,64]{0,1:T(8,128)} fusion(f32[1024,1024]{1,0:T(8,128)} %bitcast.33, f32[1024,64]{0,1:T(8,128)} %get-tuple-element.203, s32[1024]{0:T(1024)S(1)} %dynamic_slice.41, pred[]{:T(512)S(6)} %compare.4), kind=kOutput, calls=%fused_computation.2.clone.1 | convolution fusion | flops 805502976 | bytes 4722689 | tf_op jit(solution)/shard_map/while/body/eval_jaxpr/dot_general | solution.py:91
  181.4 3.0 multiply_reduce_fusion.2
  184.4 5.2 %convolution_add_fusion.2 = f32[1024,64]{0,1:T(8,128)} fusion(f32[1024,1024]{1,0:T(8,128)} %bitcast.33, f32[1024,64]{0,1:T(8,128)} %get-tuple-element.203, s32[1024]{0:T(1024)S(1)} %dynamic_slice.41, pred[]{:T(512)S(6)} %compare.4), kind=kOutput, calls=%fused_computation.2.clone.1 | convolution fusion | flops 805502976 | bytes 4722689 | tf_op jit(solution)/shard_map/while/body/eval_jaxpr/dot_general | solution.py:91
  190.8 3.0 multiply_reduce_fusion.2
  193.8 5.2 %convolution_add_fusion.2 = f32[1024,64]{0,1:T(8,128)} fusion(f32[1024,1024]{1,0:T(8,128)} %bitcast.33, f32[1024,64]{0,1:T(8,128)} %get-tuple-element.203, s32[1024]{0:T(1024)S(1)} %dynamic_slice.41, pred[]{:T(512)S(6)} %compare.4), kind=kOutput, calls=%fused_computation.2.clone.1 | convolution fusion | flops 805502976 | bytes 4722689 | tf_op jit(solution)/shard_map/while/body/eval_jaxpr/dot_general | solution.py:91
  200.1 3.0 multiply_reduce_fusion.2
  203.1 5.2 %convolution_add_fusion.2 = f32[1024,64]{0,1:T(8,128)} fusion(f32[1024,1024]{1,0:T(8,128)} %bitcast.33, f32[1024,64]{0,1:T(8,128)} %get-tuple-element.203, s32[1024]{0:T(1024)S(1)} %dynamic_slice.41, pred[]{:T(512)S(6)} %compare.4), kind=kOutput, calls=%fused_computation.2.clone.1 | convolution fusion | flops 805502976 | bytes 4722689 | tf_op jit(solution)/shard_map/while/body/eval_jaxpr/dot_general | solution.py:91
  209.5 3.0 multiply_reduce_fusion.2
  212.5 5.2 %convolution_add_fusion.2 = f32[1024,64]{0,1:T(8,128)} fusion(f32[1024,1024]{1,0:T(8,128)} %bitcast.33, f32[1024,64]{0,1:T(8,128)} %get-tuple-element.203, s32[1024]{0:T(1024)S(1)} %dynamic_slice.41, pred[]{:T(512)S(6)} %compare.4), kind=kOutput, calls=%fused_computation.2.clone.1 | convolution fusion | flops 805502976 | bytes 4722689 | tf_op jit(solution)/shard_map/while/body/eval_jaxpr/dot_general | solution.py:91
  218.8 3.0 multiply_reduce_fusion.2
  221.8 5.2 %convolution_add_fusion.2 = f32[1024,64]{0,1:T(8,128)} fusion(f32[1024,1024]{1,0:T(8,128)} %bitcast.33, f32[1024,64]{0,1:T(8,128)} %get-tuple-element.203, s32[1024]{0:T(1024)S(1)} %dynamic_slice.41, pred[]{:T(512)S(6)} %compare.4), kind=kOutput, calls=%fused_computation.2.clone.1 | convolution fusion | flops 805502976 | bytes 4722689 | tf_op jit(solution)/shard_map/while/body/eval_jaxpr/dot_general | solution.py:91
  231.2 5.2 %convolution_add_fusion.2 = f32[1024,64]{0,1:T(8,128)} fusion(f32[1024,1024]{1,0:T(8,128)} %bitcast.33, f32[1024,64]{0,1:T(8,128)} %get-tuple-element.203, s32[1024]{0:T(1024)S(1)} %dynamic_slice.41, pred[]{:T(512)S(6)} %compare.4), kind=kOutput, calls=%fused_computation.2.clone.1 | convolution fusion | flops 805502976 | bytes 4722689 | tf_op jit(solution)/shard_map/while/body/eval_jaxpr/dot_general | solution.py:91
  240.5 5.2 %convolution_add_fusion.2 = f32[1024,64]{0,1:T(8,128)} fusion(f32[1024,1024]{1,0:T(8,128)} %bitcast.33, f32[1024,64]{0,1:T(8,128)} %get-tuple-element.203, s32[1024]{0:T(1024)S(1)} %dynamic_slice.41, pred[]{:T(512)S(6)} %compare.4), kind=kOutput, calls=%fused_computation.2.clone.1 | convolution fusion | flops 805502976 | bytes 4722689 | tf_op jit(solution)/shard_map/while/body/eval_jaxpr/dot_general | solution.py:91
  249.9 5.2 %convolution_add_fusion.2 = f32[1024,64]{0,1:T(8,128)} fusion(f32[1024,1024]{1,0:T(8,128)} %bitcast.33, f32[1024,64]{0,1:T(8,128)} %get-tuple-element.203, s32[1024]{0:T(1024)S(1)} %dynamic_slice.41, pred[]{:T(512)S(6)} %compare.4), kind=kOutput, calls=%fused_computation.2.clone.1 | convolution fusion | flops 805502976 | bytes 4722689 | tf_op jit(solution)/shard_map/while/body/eval_jaxpr/dot_general | solution.py:91
  259.3 5.2 %convolution_add_fusion.2 = f32[1024,64]{0,1:T(8,128)} fusion(f32[1024,1024]{1,0:T(8,128)} %bitcast.33, f32[1024,64]{0,1:T(8,128)} %get-tuple-element.203, s32[1024]{0:T(1024)S(1)} %dynamic_slice.41, pred[]{:T(512)S(6)} %compare.4), kind=kOutput, calls=%fused_computation.2.clone.1 | convolution fusion | flops 805502976 | bytes 4722689 | tf_op jit(solution)/shard_map/while/body/eval_jaxpr/dot_general | solution.py:91
  268.6 5.2 %convolution_add_fusion.2 = f32[1024,64]{0,1:T(8,128)} fusion(f32[1024,1024]{1,0:T(8,128)} %bitcast.33, f32[1024,64]{0,1:T(8,128)} %get-tuple-element.203, s32[1024]{0:T(1024)S(1)} %dynamic_slice.41, pred[]{:T(512)S(6)} %compare.4), kind=kOutput, calls=%fused_computation.2.clone.1 | convolution fusion | flops 805502976 | bytes 4722689 | tf_op jit(solution)/shard_map/while/body/eval_jaxpr/dot_general | solution.py:91
  278.0 5.2 %convolution_add_fusion.2 = f32[1024,64]{0,1:T(8,128)} fusion(f32[1024,1024]{1,0:T(8,128)} %bitcast.33, f32[1024,64]{0,1:T(8,128)} %get-tuple-element.203, s32[1024]{0:T(1024)S(1)} %dynamic_slice.41, pred[]{:T(512)S(6)} %compare.4), kind=kOutput, calls=%fused_computation.2.clone.1 | convolution fusion | flops 805502976 | bytes 4722689 | tf_op jit(solution)/shard_map/while/body/eval_jaxpr/dot_general | solution.py:91
  287.3 5.2 %convolution_add_fusion.2 = f32[1024,64]{0,1:T(8,128)} fusion(f32[1024,1024]{1,0:T(8,128)} %bitcast.33, f32[1024,64]{0,1:T(8,128)} %get-tuple-element.203, s32[1024]{0:T(1024)S(1)} %dynamic_slice.41, pred[]{:T(512)S(6)} %compare.4), kind=kOutput, calls=%fused_computation.2.clone.1 | convolution fusion | flops 805502976 | bytes 4722689 | tf_op jit(solution)/shard_map/while/body/eval_jaxpr/dot_general | solution.py:91
  293.7 3.0 multiply_reduce_fusion.2
  296.7 5.2 %convolution_add_fusion.2 = f32[1024,64]{0,1:T(8,128)} fusion(f32[1024,1024]{1,0:T(8,128)} %bitcast.33, f32[1024,64]{0,1:T(8,128)} %get-tuple-element.203, s32[1024]{0:T(1024)S(1)} %dynamic_slice.41, pred[]{:T(512)S(6)} %compare.4), kind=kOutput, calls=%fused_computation.2.clone.1 | convolution fusion | flops 805502976 | bytes 4722689 | tf_op jit(solution)/shard_map/while/body/eval_jaxpr/dot_general | solution.py:91
  301.9 3.6 %all-to-all-start = ((f32[8,8,1024]{2,1,0:T(8,128)}), f32[8,8,1024]{2,1,0:T(8,128)S(1)}, u32[]{:S(2)}, u32[]{:S(2)}) async-start(f32[8,8,1024]{2,1,0:T(8,128)} %bitcast.5), calls=%async_computation | async-start | bytes 524288 | tf_op jit(solution)/shard_map/all_to_all | solution.py:98
  305.7 6.8 %all-to-all-done = f32[8,8,1024]{2,1,0:T(8,128)S(1)} async-done(((f32[8,8,1024]{2,1,0:T(8,128)}), f32[8,8,1024]{2,1,0:T(8,128)S(1)}, u32[]{:S(2)}, u32[]{:S(2)}) %all-to-all-start) | async-done | bytes 262176 | tf_op jit(solution)/shard_map/all_to_all | solution.py:98
  (103 shorter events, 62.7 us)
Async XLA Ops:
  6.5 14.4 %copy-start = (s32[8,8,8]{2,1,0:T(8,128)S(1)}, s32[8,8,8]{2,1,0:T(8,128)}, u32[]{:S(2)}) copy-start(s32[8,8,8]{2,1,0:T(8,128)} %param.9) | copy-start | bytes 6148
  6.5 135.3 %all-gather.2.cloned.1.call-start = ((), (), s32[]{:S(2)}) async-start(), calls=%async_computation.1 | async-start | bytes 7864320 | tf_op jit(solution)/shard_map/all_gather | solution.py:72
  8.0 3.7 %collective-permute-start = (bf16[16,1,2048]{2,1,0:T(2,128)(2,1)S(1)}, bf16[16,1,2048]{2,1,0:T(2,128)(2,1)S(1)}, u32[]{:S(2)}, u32[]{:S(2)}) collective-permute-start(bf16[16,1,2048]{2,1,0:T(2,128)(2,1)S(1)} %get-tuple-element.160), channel_id=1, source_target_pairs={{0,4},{4,8},{8,12},{12,16},{16,20},{20,24},{24,28},{1,5},{5,9},{9,... | collective-permute-start | bytes 196616 | tf_op jit(solution)/shard_map/ppermute | solution.py:23
  10.3 5.3 %collective-permute-start.1 = (bf16[16,1,2048]{2,1,0:T(2,128)(2,1)S(1)}, bf16[16,1,2048]{2,1,0:T(2,128)(2,1)S(1)}, u32[]{:S(2)}, u32[]{:S(2)}) collective-permute-start(bf16[16,1,2048]{2,1,0:T(2,128)(2,1)S(1)} %get-tuple-element.161), channel_id=1, source_target_pairs={{4,0},{8,4},{12,8},{16,12},{20,16},{24,20},{28,24},{5,1},{9,5},{13... | collective-permute-start | bytes 196616 | tf_op jit(solution)/shard_map/ppermute | solution.py:25
  19.1 1.7 copy-start.1
  19.1 1.7 copy-start.3
  19.1 1.7 copy-start.5
  19.1 1.7 copy-start.9
  19.2 1.9 copy-start.8
  23.4 5.6 %copy-start.2 = (bf16[1,16,8,2048]{3,2,1,0:T(8,128)(2,1)S(1)}, bf16[1,16,8,2048]{3,2,1,0:T(8,128)(2,1)}, u32[]{:S(2)}) copy-start(bf16[1,16,8,2048]{3,2,1,0:T(8,128)(2,1)} %copy-done.1) | copy-start | bytes 1572868
  23.4 5.6 %copy-start.4 = (bf16[1,16,8,2048]{3,2,1,0:T(8,128)(2,1)S(1)}, bf16[1,16,8,2048]{3,2,1,0:T(8,128)(2,1)}, u32[]{:S(2)}) copy-start(bf16[1,16,8,2048]{3,2,1,0:T(8,128)(2,1)} %copy-done.3) | copy-start | bytes 1572868
  23.4 5.6 %copy-start.6 = (bf16[1,16,8,2048]{3,2,1,0:T(8,128)(2,1)S(1)}, bf16[1,16,8,2048]{3,2,1,0:T(8,128)(2,1)}, u32[]{:S(2)}) copy-start(bf16[1,16,8,2048]{3,2,1,0:T(8,128)(2,1)} %copy-done.5) | copy-start | bytes 1572868
  23.4 5.6 %copy-start.7 = (f32[1,16,8,2048]{3,2,1,0:T(8,128)S(1)}, f32[1,16,8,2048]{3,2,1,0:T(8,128)}, u32[]{:S(2)}) copy-start(f32[1,16,8,2048]{3,2,1,0:T(8,128)} %get-tuple-element.146) | copy-start | bytes 3145732
  301.9 10.5 %all-to-all-start = ((f32[8,8,1024]{2,1,0:T(8,128)}), f32[8,8,1024]{2,1,0:T(8,128)S(1)}, u32[]{:S(2)}, u32[]{:S(2)}) async-start(f32[8,8,1024]{2,1,0:T(8,128)} %bitcast.5), calls=%async_computation | async-start | bytes 524288 | tf_op jit(solution)/shard_map/all_to_all | solution.py:98
Sparse Core Ops, SparseCore 0:
  21.0 120.7 all-gather.1
where the time goes:
time: 323 us; the launch traced here: 322 us
  matrix products  84.8 us (26%)
  other arithmetic  76.4 us (24%)
  waiting for transfers between devices  68.4 us (21%)
  blocking collectives  51.6 us (16%)
  local copies, waits for them, and re-layouts  19.3 us (6%)
  between operations  13.6 us (4%)
  starting transfers between devices  7.27 us (2%)
    dot_general x16, matrix products, one_block(): jnp.dot(products, member_block, precision=lax.Precision.HIGHEST)  83.9 us
    all_gather x1, waiting for transfers between devices, per_device(): gathered_bend = lax.all_gather(own_bending, 'mode', axis=1, tiled=True)  57.6 us
    psum x1, blocking collectives, per_device(): totals = 0.5 * lax.psum(placed_sums, ('tile', 'mode'))  51.6 us
    reduce_sum x16, other arithmetic, one_block(): jnp.sum(left_block[:, :, None, :] * right_block[:, None, :, :], axis=0)  48.1 us
    convert_element_type x16, other arithmetic, one_block(): lax.dynamic_slice_in_dim(right_flat, first_node, block_nodes, 2)  17 us
    reshape x1, local copies, waits for them, and re-layouts, per_device(): right_flat = gathered_bend.reshape(3, mode_count, node_count)  10.5 us
    all_to_all x1, waiting for transfers between devices, per_device(): lax.all_to_all(routed, 'tile', split_axis=0, concat_axis=0, tiled=True)  6.77 us
  transfers between devices with their start and end apart: 4, of which 3 were waited for; matrix products, arithmetic and copies ran while one was open for 4% of the time, Pallas kernels for 0%

commit v1 on v0

v1 whole, which is shorter than its diff:
```python
import functools

import jax
import jax.numpy as jnp
from jax import lax
from jax.experimental import pallas as pl
from jax.experimental.pallas import tpu as pltpu
from jax.sharding import PartitionSpec as P

ZONES = 512
POISSON = 0.3
SHEAR = 2.0 * (1.0 - POISSON)
LANES = 128


def bend_row(frame_ref, row, first_col, last_col):
    up = frame_ref[row].astype(jnp.float32)
    mid = frame_ref[row + 1].astype(jnp.float32)
    down = frame_ref[row + 2].astype(jnp.float32)
    width = mid.shape[1]

    def before(cells):
        return jnp.where(first_col, 0.0, pltpu.roll(cells, 1, 1))

    def after(cells):
        return jnp.where(last_col, 0.0, pltpu.roll(cells, width - 1, 1))

    along_x = down - 2.0 * mid + up
    along_y = after(mid) - 2.0 * mid + before(mid)
    slope = down - up
    twist = 0.25 * (after(slope) - before(slope))
    return [c.astype(jnp.bfloat16) for c in (along_x, along_y, twist)]


def pair_kernel(owners, entries, a_ref, b_ref, stiff_ref, slot_ref, acc_ref, sums_ref, left_s, right_s):
    rows = stiff_ref.shape[0]
    panel, width = a_ref.shape[1:]
    column = lax.broadcasted_iota(jnp.int32, (panel, width), 1)
    first_col = column == 0
    last_col = column == width - 1
    acc_ref[...] = jnp.zeros_like(acc_ref)
    sums_ref[...] = jnp.zeros_like(sums_ref)

    def one_row(row, carry):
        stiff = stiff_ref[row]
        slot = slot_ref[row]
        owner = slot // entries
        entry = slot - owner * entries
        owner_b = jnp.broadcast_to(owner, (panel, width))
        entry_b = jnp.broadcast_to(entry, (panel, width))
        lefts, rights = [], []
        for number, ref in enumerate((a_ref, b_ref)):
            bend = bend_row(ref, row, first_col, last_col)
            bx, by, bt = [c.astype(jnp.float32) for c in bend]
            lx = stiff * (bx + POISSON * by)
            ly = stiff * (by + POISSON * bx)
            lt = stiff * (SHEAR * bt)
            if number == 0:
                inside = jnp.sum(lx * bx + ly * by + lt * bt, axis=1, keepdims=True)
                sums_ref[...] += jnp.broadcast_to(inside, sums_ref.shape)
            rights.append(bend)
            lefts.append([c.astype(jnp.bfloat16) for c in (lx, ly, lt)])
        for k in range(owners):
            mask = (owner_b == k).astype(jnp.float32).astype(jnp.bfloat16)
            for c in range(3):
                for n in range(2):
                    left_s[c, pl.ds((n * owners + k) * panel, panel), :] = lefts[n][c] * mask
        for k in range(entries):
            mask = (entry_b == k).astype(jnp.float32).astype(jnp.bfloat16)
            for c in range(3):
                for n in range(2):
                    right_s[c, pl.ds((n * entries + k) * panel, panel), :] = rights[n][c] * mask
        for c in range(3):
            acc_ref[...] += lax.dot_general(
                left_s[c], right_s[c], (((1,), (1,)), ((), ())), preferred_element_type=jnp.float32
            )
        return carry

    lax.fori_loop(0, rows, one_row, 0)


def pair_sums(own, other, stiff, slot, owners, entries):
    rows = stiff.shape[0]
    panel, width = own.shape[1:]
    tall, wide = 2 * owners * panel, 2 * entries * panel
    whole = pl.BlockSpec(memory_space=pltpu.VMEM)
    return pl.pallas_call(
        functools.partial(pair_kernel, owners, entries),
        out_shape=(
            jax.ShapeDtypeStruct((tall, wide), jnp.float32),
            jax.ShapeDtypeStruct((panel, LANES), jnp.float32),
        ),
        in_specs=[whole] * 4,
        out_specs=(whole, whole),
        scratch_shapes=[
            pltpu.VMEM((3, tall, width), jnp.bfloat16),
            pltpu.VMEM((3, wide, width), jnp.bfloat16),
        ],
        compiler_params=pltpu.CompilerParams(vmem_limit_bytes=48 << 20),
        cost_estimate=pl.CostEstimate(
            flops=2 * 3 * tall * wide * rows * width,
            bytes_accessed=4 * rows * panel * width * 2,
            transcendentals=0,
        ),
    )(own, other, stiff.reshape(rows, 1, width), slot.reshape(rows, 1, width))


def zone_kernel(place_ref, source_ref, blocks_ref, scale_ref, out_ref):
    panels, tiles, panel, _ = blocks_ref.shape
    entries = source_ref.shape[1]
    me = place_ref[0]
    out_ref[...] = jnp.zeros_like(out_ref)
    scale = scale_ref[...]

    def one_tile(tile, carry):
        got = [blocks_ref[lax.rem(g - me + panels, panels), tile] for g in range(panels)]
        for k in range(entries):
            row = jnp.concatenate([b[:, k * panel : (k + 1) * panel] for b in got], axis=1)
            zone = source_ref[tile, k]
            out_ref[zone] += row * scale
        return carry

    lax.fori_loop(0, tiles, one_tile, 0)


def per_device(mode_shapes, stiffness, node_slot, slot_zone):
    panel, rows, width = mode_shapes.shape
    tiles = lax.axis_size("tile")
    panels = lax.axis_size("mode")
    modes = panel * panels
    entries = slot_zone.shape[2]
    owned = ZONES // tiles
    me = lax.axis_index("mode")
    tile = lax.axis_index("tile")
    half = panels // 2

    own = mode_shapes.transpose(1, 0, 2)
    below = lax.ppermute(own[-1:], "tile", [(i, i + 1) for i in range(tiles - 1)])
    above = lax.ppermute(own[:1], "tile", [(i + 1, i) for i in range(tiles - 1)])
    frame = jnp.concatenate([below, own, above], axis=0)

    part = width // 2 + LANES
    shift = width // 2 - LANES
    mine_start = jnp.where(me < half, 0, shift)
    their_start = jnp.where(me < half, shift, 0)
    sent_half = lax.dynamic_slice_in_dim(frame, their_start, part, 2)
    others = [
        lax.ppermute(frame, "mode", [(i, (i - d) % panels) for i in range(panels)]) for d in range(1, half)
    ]
    other_half = lax.ppermute(sent_half, "mode", [(i, (i - half) % panels) for i in range(panels)])

    blocks = [None] * panels
    for d in range(1, half):
        acc, sums = pair_sums(frame, others[d - 1], stiffness, node_slot, tiles, entries)
        if d == 1:
            own_sums = sums[:, 0]
            blocks[0] = acc[: tiles * panel, : entries * panel]
        blocks[d] = acc[: tiles * panel, entries * panel :]
        blocks[panels - d] = lax.ppermute(
            acc[tiles * panel :, : entries * panel], "mode", [(i, (i + d) % panels) for i in range(panels)]
        )
    placed = lax.dynamic_update_slice_in_dim(jnp.zeros((modes,), jnp.float32), own_sums, me * panel, 0)
    totals = 0.5 * lax.psum(placed, ("tile", "mode"))

    own_half = lax.dynamic_slice_in_dim(frame, mine_start, part, 2)
    stiff_half = lax.dynamic_slice_in_dim(stiffness, mine_start, part, 1)
    slot_half = lax.dynamic_slice_in_dim(node_slot, mine_start, part, 1)
    column = jnp.arange(part)[None, :]
    inside = jnp.where(me < half, column < width // 2, column >= LANES)
    slot_half = jnp.where(inside, slot_half, tiles * entries)
    acc, _ = pair_sums(own_half, other_half, stiff_half, slot_half, tiles, entries)
    returned = lax.ppermute(
        acc[tiles * panel :, : entries * panel], "mode", [(i, (i + half) % panels) for i in range(panels)]
    )
    blocks[half] = acc[: tiles * panel, entries * panel :] + returned

    stacked = jnp.stack(blocks).reshape(panels, tiles, panel, entries * panel)
    arrived = lax.all_to_all(stacked, "tile", split_axis=1, concat_axis=1, tiled=True)
    source = lax.dynamic_index_in_dim(slot_zone, tile, 1, keepdims=False)
    mine = lax.dynamic_slice_in_dim(totals, me * panel, panel, 0)
    scale = (0.5 * ZONES) / jnp.sqrt(mine[:, None] * totals[None, :])
    return pl.pallas_call(
        zone_kernel,
        out_shape=jax.ShapeDtypeStruct((owned, panel, modes), jnp.float32),
        in_specs=[
            pl.BlockSpec(memory_space=pltpu.SMEM),
            pl.BlockSpec(memory_space=pltpu.SMEM),
            pl.BlockSpec(memory_space=pltpu.VMEM),
            pl.BlockSpec(memory_space=pltpu.VMEM),
        ],
        out_specs=pl.BlockSpec(memory_space=pltpu.VMEM),
    )(me.reshape(1), source, arrived, scale)


def solution(mesh):
    placed = (P("mode", "tile", None), P("tile", None), P("tile", None), P())
    return jax.shard_map(
        per_device, mesh=mesh, in_specs=placed, out_specs=P("tile", "mode", None), check_vma=False
    )
```

time: 323 us -> 126 us (0.39)
  matrix products: 84.8 us -> 0 us
  other arithmetic: 76.4 us -> 1.51 us
  waiting for transfers between devices: 68.4 us -> 28.7 us
  starting transfers between devices: 7.27 us -> 29.8 us
  Pallas kernels: 0 us -> 20.5 us
  local copies, waits for them, and re-layouts: 19.3 us -> 4.17 us
  between operations: 13.6 us -> 0.19 us
  blocking collectives: 51.6 us -> 40.5 us
    dot_general x17 -> x0, matrix products: 84.8 us -> none  [the longest x16 83.9 us: one_block(): jnp.dot(products, member_block, precision=lax.Precision.HIGHEST)]
    all_gather x1 -> x0, waiting for transfers between devices: 57.6 us -> none  [per_device(): gathered_bend = lax.all_gather(own_bending, 'mode', axis=1, tiled=True)]
    reduce_sum x17 -> x0, other arithmetic: 50.1 us -> none  [the longest x16 48.1 us: one_block(): jnp.sum(left_block[:, :, None, :] * right_block[:, None, :, :], axis=0)]
    ppermute x2 -> x6, starting transfers between devices: 3.66 us -> 24.8 us  [the longest x1 15 us: per_device(): lax.ppermute(acc[tiles * panel:, :entries * panel], 'mode', [(i, (i + d)...]
    pallas_call x0 -> x3, Pallas kernels: none -> 20.5 us  [the longest x2 17.6 us: pair_sums(): pl.pallas_call(functools.partial(pair_kernel, owners, entries), out_shape...]
    convert_element_type x33 -> x0, other arithmetic: 18.9 us -> none  [the longest x16 17 us: one_block(): lax.dynamic_slice_in_dim(right_flat, first_node, block_nodes, 2)]
    ppermute x2 -> x6, waiting for transfers between devices: 4.03 us -> 22.5 us  [the longest x1 15.3 us: per_device(): lax.ppermute(sent_half, 'mode', [(i, (i - half) % panels) for i in range(...]
    psum x1, blocking collectives: 51.6 us -> 40.5 us  [per_device(): totals = 0.5 * lax.psum(placed, ('tile', 'mode'))]
  transfers between devices with their start and end apart: 4 -> 7, of which waited for: 3 -> 3; matrix products, arithmetic and copies ran while one was open for 4% -> 2% of each run, Pallas kernels for 0% -> 6%
where the time goes in v1:
time: 126 us; the launch traced here: 125 us
  blocking collectives  40.5 us (32%)
  starting transfers between devices  29.8 us (24%)
  waiting for transfers between devices  28.7 us (23%)
  Pallas kernels  20.5 us (16%)
  local copies, waits for them, and re-layouts  4.17 us (3%)
  other arithmetic  1.51 us (1%)
    psum x1, blocking collectives, per_device(): totals = 0.5 * lax.psum(placed, ('tile', 'mode'))  40.5 us
    pallas_call x2, Pallas kernels, pair_sums(): pl.pallas_call(functools.partial(pair_kernel, owners, entries), out_shape...  17.6 us
    ppermute x1, waiting for transfers between devices, per_device(): lax.ppermute(sent_half, 'mode', [(i, (i - half) % panels) for i in range(...  15.3 us
    ppermute x1, starting transfers between devices, per_device(): lax.ppermute(acc[tiles * panel:, :entries * panel], 'mode', [(i, (i + d)...  15 us
    ppermute x1, waiting for transfers between devices, per_device(): lax.ppermute(acc[tiles * panel:, :entries * panel], 'mode', [(i, (i + hal...  7.25 us
    all_to_all x1, waiting for transfers between devices, per_device(): lax.all_to_all(stacked, 'tile', split_axis=1, concat_axis=1, tiled=True)  6.17 us
    all_to_all x1, starting transfers between devices, per_device(): lax.all_to_all(stacked, 'tile', split_axis=1, concat_axis=1, tiled=True)  4.97 us
    ppermute x1, starting transfers between devices, per_device(): lax.ppermute(sent_half, 'mode', [(i, (i - half) % panels) for i in range(...  4.1 us
  transfers between devices with their start and end apart: 7, of which 3 were waited for; matrix products, arithmetic and copies ran while one was open for 2% of the time, Pallas kernels for 6%

profile of v1, /device:TPU:0, one launch (start us, length us, event | category | flops | bytes accessed | tf_op | source)
XLA Modules:
  0.0 125.4 jit_solution(120228289415646093)
XLA Ops:
  0.0 0.0 copy-start
  0.0 1.3 %copy.18 = bf16[16,8,2048]{2,0,1:T(8,128)(2,1)S(1)} copy(bf16[16,8,2048]{2,1,0:T(8,128)(2,1)} %param.4) | data formatting | bytes 1048576 | tf_op args[0]
  1.3 0.0 copy-start.1
  1.4 1.3 %collective-permute-start.1 = (bf16[1,16,2048]{2,1,0:T(8,128)(2,1)S(1)}, bf16[1,16,2048]{2,1,0:T(8,128)(2,1)S(1)}, u32[]{:S(2)}, u32[]{:S(2)}) collective-permute-start(bf16[1,16,2048]{2,1,0:T(8,128)(2,1)S(1)} %get-tuple-element.14), channel_id=1, source_target_pairs={{4,0},{8,4},{12,8},{16,12},{20,16},{24,20},{28,24},{5,1},{9,5},{13... | collective-permute-start | bytes 196616 | tf_op jit(solution)/shard_map/ppermute | solution.py:139
  2.7 3.0 %collective-permute-start = (bf16[1,16,2048]{2,1,0:T(8,128)(2,1)S(1)}, bf16[1,16,2048]{2,1,0:T(8,128)(2,1)S(1)}, u32[]{:S(2)}, u32[]{:S(2)}) collective-permute-start(bf16[1,16,2048]{2,1,0:T(8,128)(2,1)S(1)} %get-tuple-element.13), channel_id=1, source_target_pairs={{0,4},{4,8},{8,12},{12,16},{16,20},{20,24},{24,28},{1,5},{5,9},{9,... | collective-permute-start | bytes 196616 | tf_op jit(solution)/shard_map/ppermute | solution.py:138
  5.7 0.0 copy-start.2
  5.8 0.8 copy-done.2
  6.7 0.0 collective-permute-done.1
  6.7 0.0 collective-permute-done
  6.7 0.1 pad_maximum_fusion.a_ref
  6.8 0.1 constant_dynamic-slice_fusion.1
  6.9 4.1 %collective-permute-start.3 = (bf16[10,16,1152]{2,1,0:T(8,128)(2,1)S(1)}, bf16[10,16,1152]{2,1,0:T(8,128)(2,1)S(1)}, u32[]{:S(2)}, u32[]{:S(2)}) collective-permute-start(bf16[10,16,1152]{2,1,0:T(8,128)(2,1)S(1)} %get-tuple-element.11), channel_id=1, source_target_pairs={{0,2},{1,3},{2,0},{3,1},{4,6},{5,7},{6,4},{7,5},{8,10},{9,11},{10,... | collective-permute-start | bytes 1105928 | tf_op jit(solution)/shard_map/ppermute | solution.py:150
  11.1 1.4 %collective-permute-start.2 = (bf16[10,16,2048]{2,1,0:T(8,128)(2,1)S(1)}, bf16[10,16,2048]{2,1,0:T(8,128)(2,1)S(1)}, u32[]{:S(2)}, u32[]{:S(2)}) collective-permute-start(bf16[10,16,2048]{2,1,0:T(8,128)(2,1)S(1)} %pad_maximum_fusion.a_ref), channel_id=1, source_target_pairs={{0,3},{1,0},{2,1},{3,2},{4,7},{5,4},{6,5},{7,6},{8,11},{9,8},{10,9... | collective-permute-start | bytes 1966088 | tf_op jit(solution)/shard_map/ppermute | solution.py:148
  12.5 15.3 %collective-permute-done.3.b_ref = bf16[10,16,1152]{2,1,0:T(8,128)(2,1)S(1)} collective-permute-done((bf16[10,16,1152]{2,1,0:T(8,128)(2,1)S(1)}, bf16[10,16,1152]{2,1,0:T(8,128)(2,1)S(1)}, u32[]{:S(2)}, u32[]{:S(2)}) %collective-permute-start.3) | collective-permute-done | bytes 368672 | tf_op jit(solution)/shard_map/ppermute | solution.py:150
  27.7 7.5 %shard_map.47 = (f32[256,256]{1,0:T(8,128)S(1)}, f32[16,128]{1,0:T(8,128)}) custom-call(bf16[10,16,1152]{2,1,0:T(8,128)(2,1)S(1)} %get-tuple-element.12.a_ref, bf16[10,16,1152]{2,1,0:T(8,128)(2,1)S(1)} %collective-permute-done.3.b_ref, f32[8,1,1152]{2,1,0:T(1,128)S(1)} %reshape.40.stiff_ref, s32[8,1,1152]{2,1,0:T(1,128)S(1)} %reshape.41.slot_ref), custom_call_target="tpu_custom_call" | custom-call | flops 3623878656 | bytes 1179648 | tf_op jit(solution)/shard_map/pallas_call | solution.py:87
  35.2 0.0 collective-permute-start.4
  35.3 0.6 constant_dynamic-slice_fusion.3
  35.9 7.2 %collective-permute-done.4 = f32[128,128]{1,0:T(8,128)S(1)} collective-permute-done((f32[128,128]{1,0:T(8,128)S(1)}, f32[128,128]{1,0:T(8,128)S(1)}, u32[]{:S(2)}, u32[]{:S(2)}) %collective-permute-start.4) | collective-permute-done | bytes 65568 | tf_op jit(solution)/shard_map/ppermute | solution.py:172
  43.1 0.0 collective-permute-done.2.b_ref
  43.1 10.1 %shard_map.46 = (f32[256,256]{1,0:T(8,128)S(1)}, f32[16,128]{1,0:T(8,128)S(1)}) custom-call(bf16[10,16,2048]{2,1,0:T(8,128)(2,1)S(1)} %pad_maximum_fusion.a_ref, bf16[10,16,2048]{2,1,0:T(8,128)(2,1)S(1)} %collective-permute-done.2.b_ref, f32[8,1,2048]{2,1,0:T(1,128)S(1)} %reshape.38.stiff_ref, s32[8,1,2048]{2,1,0:T(1,128)S(1)} %reshape.39.slot_ref), custom_call_target="tpu_custom_call" | custom-call | flops 6442450944 | bytes 2097152 | tf_op jit(solution)/shard_map/pallas_call | solution.py:87
  53.3 15.0 %collective-permute-start.5 = (f32[128,128]{1,0:T(8,128)S(1)}, f32[128,128]{1,0:T(8,128)S(1)}, u32[]{:S(2)}, u32[]{:S(2)}) collective-permute-start(f32[128,128]{1,0:T(8,128)S(1)} %get-tuple-element.16), channel_id=1, source_target_pairs={{0,1},{1,2},{2,3},{3,0},{4,5},{5,6},{6,7},{7,4},{8,9},{9,10},{10,1... | collective-permute-start | bytes 196616 | tf_op jit(solution)/shard_map/ppermute | solution.py:159
  68.3 0.1 slice_reduce_fusion
  68.4 0.2 dynamic_update_slice.3
  68.6 40.5 %psum.7 = f32[64]{0:T(128)S(1)} all-reduce(f32[64]{0:T(128)S(1)} %dynamic_update_slice.3), channel_id=1, replica_groups=mesh['tile'=8,'mode'=4] {'tile','mode'}, use_global_device_ids=true, to_apply=%region_0.1 | all-reduce | flops 64 | bytes 512 | tf_op jit(solution)/shard_map/psum | solution.py:163
  109.2 0.0 collective-permute-done.5
  109.2 0.7 pad_maximum_fusion.1
  109.9 5.0 %all-to-all-start = ((f32[4,8,16,128]{3,2,0,1:T(8,128)}), f32[4,8,16,128]{3,2,0,1:T(8,128)S(1)}, u32[]{:S(2)}, u32[]{:S(2)}) async-start(f32[4,8,16,128]{3,2,0,1:T(8,128)} %pad_maximum_fusion.1), calls=%async_computation | async-start | bytes 524288 | tf_op jit(solution)/shard_map/all_to_all | solution.py:178
  114.9 0.1 dynamic_slice.24
  115.0 0.7 rsqrt_multiply_fusion.scale_ref
  115.6 6.2 %all-to-all-done = f32[4,8,16,128]{3,2,0,1:T(8,128)S(1)} async-done(((f32[4,8,16,128]{3,2,0,1:T(8,128)}), f32[4,8,16,128]{3,2,0,1:T(8,128)S(1)}, u32[]{:S(2)}, u32[]{:S(2)}) %all-to-all-start) | async-done | bytes 262176 | tf_op jit(solution)/shard_map/all_to_all | solution.py:178
  121.8 0.7 copy.15.blocks_ref
  122.5 2.8 %shard_map.48 = f32[64,16,64]{2,1,0:T(8,128)} custom-call(s32[1]{0:T(128)} %bitcast.place_ref, s32[8,8]{1,0:T(8,128)} %bitcast.25, f32[4,8,16,128]{3,2,1,0:T(8,128)} %copy.15.blocks_ref, f32[16,64]{1,0:T(8,128)} %rsqrt_multiply_fusion.scale_ref), custom_call_target="tpu_custom_call" | custom-call | tf_op jit(solution)/shard_map/pallas_call | solution.py:182
  (15 shorter events, 0.2 us)
Async XLA Ops:
  0.0 35.2 %copy-start = (s32[8,8,8]{2,1,0:T(8,128)S(1)}, s32[8,8,8]{2,1,0:T(8,128)}, u32[]{:S(2)}) copy-start(s32[8,8,8]{2,1,0:T(8,128)} %param.7) | copy-start | bytes 6148
  1.3 4.4 %copy-start.1 = (f32[8,2048]{1,0:T(8,128)S(1)}, f32[8,2048]{1,0:T(8,128)}, u32[]{:S(2)}) copy-start(f32[8,2048]{1,0:T(8,128)} %param.5) | copy-start | bytes 196612
  1.4 5.3 %collective-permute-start.1 = (bf16[1,16,2048]{2,1,0:T(8,128)(2,1)S(1)}, bf16[1,16,2048]{2,1,0:T(8,128)(2,1)S(1)}, u32[]{:S(2)}, u32[]{:S(2)}) collective-permute-start(bf16[1,16,2048]{2,1,0:T(8,128)(2,1)S(1)} %get-tuple-element.14), channel_id=1, source_target_pairs={{4,0},{8,4},{12,8},{16,12},{20,16},{24,20},{28,24},{5,1},{9,5},{13... | collective-permute-start | bytes 196616 | tf_op jit(solution)/shard_map/ppermute | solution.py:139
  2.7 4.0 %collective-permute-start = (bf16[1,16,2048]{2,1,0:T(8,128)(2,1)S(1)}, bf16[1,16,2048]{2,1,0:T(8,128)(2,1)S(1)}, u32[]{:S(2)}, u32[]{:S(2)}) collective-permute-start(bf16[1,16,2048]{2,1,0:T(8,128)(2,1)S(1)} %get-tuple-element.13), channel_id=1, source_target_pairs={{0,4},{4,8},{8,12},{12,16},{16,20},{20,24},{24,28},{1,5},{5,9},{9,... | collective-permute-start | bytes 196616 | tf_op jit(solution)/shard_map/ppermute | solution.py:138
  5.7 0.8 copy-start.2
  6.9 20.8 %collective-permute-start.3 = (bf16[10,16,1152]{2,1,0:T(8,128)(2,1)S(1)}, bf16[10,16,1152]{2,1,0:T(8,128)(2,1)S(1)}, u32[]{:S(2)}, u32[]{:S(2)}) collective-permute-start(bf16[10,16,1152]{2,1,0:T(8,128)(2,1)S(1)} %get-tuple-element.11), channel_id=1, source_target_pairs={{0,2},{1,3},{2,0},{3,1},{4,6},{5,7},{6,4},{7,5},{8,10},{9,11},{10,... | collective-permute-start | bytes 1105928 | tf_op jit(solution)/shard_map/ppermute | solution.py:150
  11.1 32.1 %collective-permute-start.2 = (bf16[10,16,2048]{2,1,0:T(8,128)(2,1)S(1)}, bf16[10,16,2048]{2,1,0:T(8,128)(2,1)S(1)}, u32[]{:S(2)}, u32[]{:S(2)}) collective-permute-start(bf16[10,16,2048]{2,1,0:T(8,128)(2,1)S(1)} %pad_maximum_fusion.a_ref), channel_id=1, source_target_pairs={{0,3},{1,0},{2,1},{3,2},{4,7},{5,4},{6,5},{7,6},{8,11},{9,8},{10,9... | collective-permute-start | bytes 1966088 | tf_op jit(solution)/shard_map/ppermute | solution.py:148
  35.2 7.9 %collective-permute-start.4 = (f32[128,128]{1,0:T(8,128)S(1)}, f32[128,128]{1,0:T(8,128)S(1)}, u32[]{:S(2)}, u32[]{:S(2)}) collective-permute-start(f32[128,128]{1,0:T(8,128)S(1)} %slice.29), channel_id=1, source_target_pairs={{0,2},{1,3},{2,0},{3,1},{4,6},{5,7},{6,4},{7,5},{8,10},{9,11},{10,... | collective-permute-start | bytes 196616 | tf_op jit(solution)/shard_map/ppermute | solution.py:172
  53.3 55.9 %collective-permute-start.5 = (f32[128,128]{1,0:T(8,128)S(1)}, f32[128,128]{1,0:T(8,128)S(1)}, u32[]{:S(2)}, u32[]{:S(2)}) collective-permute-start(f32[128,128]{1,0:T(8,128)S(1)} %get-tuple-element.16), channel_id=1, source_target_pairs={{0,1},{1,2},{2,3},{3,0},{4,5},{5,6},{6,7},{7,4},{8,9},{9,10},{10,1... | collective-permute-start | bytes 196616 | tf_op jit(solution)/shard_map/ppermute | solution.py:159
  109.9 11.9 %all-to-all-start = ((f32[4,8,16,128]{3,2,0,1:T(8,128)}), f32[4,8,16,128]{3,2,0,1:T(8,128)S(1)}, u32[]{:S(2)}, u32[]{:S(2)}) async-start(f32[4,8,16,128]{3,2,0,1:T(8,128)} %pad_maximum_fusion.1), calls=%async_computation | async-start | bytes 524288 | tf_op jit(solution)/shard_map/all_to_all | solution.py:178

commit v2 on v1

v2 whole, which is shorter than its diff:
```python
import functools

import jax
import jax.numpy as jnp
from jax import lax
from jax.experimental import pallas as pl
from jax.experimental.pallas import tpu as pltpu
from jax.sharding import PartitionSpec as P

ZONES = 512
POISSON = 0.3
SHEAR = 2.0 * (1.0 - POISSON)
LANES = 128


def bend_row(up, mid, down, first_col, last_col):
    up = up.astype(jnp.float32)
    mid = mid.astype(jnp.float32)
    down = down.astype(jnp.float32)
    width = mid.shape[1]

    def before(cells):
        return jnp.where(first_col, 0.0, pltpu.roll(cells, 1, 1))

    def after(cells):
        return jnp.where(last_col, 0.0, pltpu.roll(cells, width - 1, 1))

    along_x = down - 2.0 * mid + up
    along_y = after(mid) - 2.0 * mid + before(mid)
    slope = down - up
    twist = 0.25 * (after(slope) - before(slope))
    return [c.astype(jnp.bfloat16) for c in (along_x, along_y, twist)]


def pair_kernel(
    sizes, own_ref, stiff_ref, slot_ref, out_ref, total_ref,
    frames, half_frame, left_s, right_s, acc, sums, results, returned, arrived, tile_sums, mode_sums,
    halo_send, halo_recv, row_send, row_recv, back_send, back_recv, block_send, block_recv,
    tsum_send, tsum_recv, msum_send, msum_recv,
):
    tiles, panels, entries = sizes
    rows, panel, width = own_ref.shape
    half = panels // 2
    part = half_frame.shape[2]
    shift = width - part
    tall, wide = tiles * panel, entries * panel
    tile = lax.axis_index("tile")
    me = lax.axis_index("mode")

    def tile_peer(step):
        return lax.rem(tile + step, tiles)

    def mode_peer(step):
        return lax.rem(me + step, panels)

    def to(src, dst, send, recv, at_tile, at_mode):
        return pltpu.make_async_remote_copy(
            src_ref=src, dst_ref=dst, send_sem=send, recv_sem=recv,
            device_id=(at_tile, at_mode), device_id_type=pl.DeviceIdType.MESH,
        )

    barrier = pltpu.get_barrier_semaphore()
    for step in range(1, panels):
        pl.semaphore_signal(barrier, inc=1, device_id=(tile, mode_peer(step)), device_id_type=pl.DeviceIdType.MESH)

    def greet(step, carry):
        pl.semaphore_signal(barrier, inc=1, device_id=(tile_peer(step), me), device_id_type=pl.DeviceIdType.MESH)
        return carry

    lax.fori_loop(1, tiles, greet, 0)

    first_tile, last_tile = tile == 0, tile == tiles - 1

    @pl.when(first_tile)
    def _():
        for d in range(half):
            frames[d, 0] = jnp.zeros((panel, width), jnp.bfloat16)
        half_frame[0] = jnp.zeros((panel, part), jnp.bfloat16)

    @pl.when(last_tile)
    def _():
        for d in range(half):
            frames[d, rows + 1] = jnp.zeros((panel, width), jnp.bfloat16)
        half_frame[rows + 1] = jnp.zeros((panel, part), jnp.bfloat16)

    pl.semaphore_wait(barrier, panels - 1 + tiles - 1)

    their_start = pl.multiple_of(jnp.where(me < half, shift, 0), LANES)
    mine_start = pl.multiple_of(jnp.where(me < half, 0, shift), LANES)

    def row_copy(d, row):
        if d == half:
            src, dst = own_ref.at[row, :, pl.ds(their_start, part)], half_frame.at[row + 1]
        else:
            src, dst = own_ref.at[row], frames.at[d, row + 1]
        return to(src, dst, row_send.at[d, row], row_recv.at[d, row], tile, mode_peer(panels - d))

    def edge_copies(d):
        frame = half_frame if d == half else frames.at[d]
        top = own_ref.at[0] if d == 0 else frame.at[1]
        bottom = own_ref.at[rows - 1] if d == 0 else frame.at[rows]
        upward = to(top, frame.at[rows + 1], halo_send.at[d, 0], halo_recv.at[d, 0], jnp.maximum(tile - 1, 0), me)
        downward = to(
            bottom, frame.at[0], halo_send.at[d, 1], halo_recv.at[d, 1], jnp.minimum(tile + 1, tiles - 1), me
        )
        return upward, downward

    def start_edges(d):
        upward, downward = edge_copies(d)
        pl.when(jnp.logical_not(first_tile))(upward.start)
        pl.when(jnp.logical_not(last_tile))(downward.start)

    def await_edges(d):
        upward, downward = edge_copies(d)
        pl.when(jnp.logical_not(last_tile))(upward.wait_recv)
        pl.when(jnp.logical_not(first_tile))(downward.wait_recv)

    def finish_edges(d):
        upward, downward = edge_copies(d)
        pl.when(jnp.logical_not(first_tile))(upward.wait_send)
        pl.when(jnp.logical_not(last_tile))(downward.wait_send)

    start_edges(0)
    for d in range(1, half + 1):
        row_copy(d, 0).start()
        row_copy(d, rows - 1).start()
    for d in range(1, half + 1):
        for row in range(1, rows - 1):
            row_copy(d, row).start()
    for row in range(rows):
        frames[0, row + 1] = own_ref[row]

    sums[...] = jnp.zeros_like(sums)

    def block_copy(block, step):
        peer = tile_peer(step)
        return to(
            results.at[block, peer], arrived.at[block, tile],
            block_send.at[block, step], block_recv.at[block, step], peer, me,
        )

    def start_blocks(block):
        def go(step, carry):
            block_copy(block, step).start()
            return carry

        lax.fori_loop(1, tiles, go, 0)
        arrived[block, tile] = results[block, tile]

    def back_copy(d):
        block = results.at[panels + d]
        return to(block, returned.at[d], back_send.at[d], back_recv.at[d], tile, mode_peer(d))

    def tsum_copy(step):
        return to(sums, tile_sums.at[tile], tsum_send.at[step], tsum_recv.at[step], tile_peer(step), me)

    def keep(block, values):
        results[block] = values.reshape(tiles, panel, wide)

    for d in range(1, half + 1):
        split = d == half
        span = part if split else width
        column = lax.broadcasted_iota(jnp.int32, (panel, span), 1)
        first_col, last_col = column == 0, column == span - 1
        if split:
            inside = jnp.where(me < half, (column < width // 2).astype(jnp.int32), (column >= LANES).astype(jnp.int32))
        row_copy(d, 0).wait_recv()
        row_copy(d, rows - 1).wait_recv()
        start_edges(d)
        row_copy(d, 1).wait_recv()
        acc[...] = jnp.zeros_like(acc)

        def one_row(k, carry):
            row = lax.rem(k + 1, rows)

            @pl.when(k < rows - 3)
            def _():
                row_copy(d, k + 2).wait_recv()

            @pl.when(k == rows - 2)
            def _():
                if d == 1:
                    await_edges(0)
                await_edges(d)

            if split:
                here = pl.ds(mine_start, part)
                stiff, slot = stiff_ref[row, :, here], slot_ref[row, :, here]
                mine = [frames[0, row + i, :, here] for i in range(3)]
                theirs = [half_frame[row + i] for i in range(3)]
            else:
                stiff, slot = stiff_ref[row], slot_ref[row]
                mine = [frames[0, row + i] for i in range(3)]
                theirs = [frames[d, row + i] for i in range(3)]
            owner = slot // entries
            entry = slot - owner * entries
            owner_b = jnp.broadcast_to(owner, (panel, span))
            entry_b = jnp.broadcast_to(entry, (panel, span))
            if split:
                owner_b = jnp.where(inside == 1, owner_b, tiles)
            lefts, rights = [], []
            for number, taken in enumerate((mine, theirs)):
                bend = bend_row(*taken, first_col, last_col)
                bx, by, bt = [c.astype(jnp.float32) for c in bend]
                lx = stiff * (bx + POISSON * by)
                ly = stiff * (by + POISSON * bx)
                lt = stiff * (SHEAR * bt)
                if number == 0 and d == 1:
                    row_sum = jnp.sum(lx * bx + ly * by + lt * bt, axis=1, keepdims=True)
                    sums[...] += jnp.broadcast_to(row_sum, sums.shape)
                rights.append(bend)
                lefts.append([c.astype(jnp.bfloat16) for c in (lx, ly, lt)])
            for k in range(tiles):
                mask = (owner_b == k).astype(jnp.float32).astype(jnp.bfloat16)
                for c in range(3):
                    for n in range(2):
                        left_s[c, pl.ds((n * tiles + k) * panel, panel), pl.ds(0, span)] = lefts[n][c] * mask
            for k in range(entries):
                mask = (entry_b == k).astype(jnp.float32).astype(jnp.bfloat16)
                for c in range(3):
                    for n in range(2):
                        right_s[c, pl.ds((n * entries + k) * panel, panel), pl.ds(0, span)] = rights[n][c] * mask
            for c in range(3):
                acc[...] += lax.dot_general(
                    left_s[c, :, pl.ds(0, span)], right_s[c, :, pl.ds(0, span)],
                    (((1,), (1,)), ((), ())), preferred_element_type=jnp.float32,
                )
            return carry

        lax.fori_loop(0, rows, one_row, 0)
        keep(panels + d, acc[pl.ds(tall, tall), pl.ds(0, wide)])
        back_copy(d).start()
        if d == 1:

            def send_sum(step, carry):
                tsum_copy(step).start()
                return carry

            lax.fori_loop(1, tiles, send_sum, 0)
            tile_sums[tile] = sums[...]
            keep(0, acc[pl.ds(0, tall), pl.ds(0, wide)])
            start_blocks(0)
        values = acc[pl.ds(0, tall), pl.ds(wide, wide)]
        if split:
            def take_sum(step, carry):
                tsum_copy(step).wait()
                return carry

            lax.fori_loop(1, tiles, take_sum, 0)
            mode_sums[me] = jnp.sum(tile_sums[...], axis=0)
            msums = [
                to(mode_sums.at[me], mode_sums.at[me], msum_send.at[step], msum_recv.at[step], tile, mode_peer(step))
                for step in range(1, panels)
            ]
            for copy in msums:
                copy.start()
            for e in range(1, half):
                back_copy(e).wait()
                results[panels - e] = returned[e]
                start_blocks(panels - e)
            back_copy(d).wait()
            keep(half, values)
            results[half] += returned[half]
            start_blocks(half)
        else:
            keep(d, values)
            start_blocks(d)

    for d in range(half + 1):
        finish_edges(d)
    for d in range(1, half + 1):
        for row in range(rows):
            row_copy(d, row).wait_send()
    for copy in msums:
        copy.wait()

    for block in range(panels):
        def take(step, carry):
            block_copy(block, step).wait()
            return carry

        lax.fori_loop(1, tiles, take, 0)
    out_ref[...] = arrived[...]
    total_ref[...] = mode_sums[...]


def pair_sums(own, stiff, slot, tiles, panels, entries):
    rows, panel, width = own.shape
    half = panels // 2
    part = width // 2 + LANES
    tall, wide = 2 * tiles * panel, 2 * entries * panel
    whole = pl.BlockSpec(memory_space=pltpu.VMEM)
    blocks = (panels, tiles, panel, entries * panel)
    dma = pltpu.SemaphoreType.DMA
    f32, bf16 = jnp.float32, jnp.bfloat16
    return pl.pallas_call(
        functools.partial(pair_kernel, (tiles, panels, entries)),
        out_shape=(
            jax.ShapeDtypeStruct(blocks, f32),
            jax.ShapeDtypeStruct((panels, panel, LANES), f32),
        ),
        in_specs=[whole] * 3,
        out_specs=(whole, whole),
        scratch_shapes=[
            pltpu.VMEM((half, rows + 2, panel, width), bf16),
            pltpu.VMEM((rows + 2, panel, part), bf16),
            pltpu.VMEM((3, tall, width), bf16),
            pltpu.VMEM((3, wide, width), bf16),
            pltpu.VMEM((tall, wide), f32),
            pltpu.VMEM((panel, LANES), f32),
            pltpu.VMEM((panels + half + 1,) + blocks[1:], f32),
            pltpu.VMEM((half + 1,) + blocks[1:], f32),
            pltpu.VMEM(blocks, f32),
            pltpu.VMEM((tiles, panel, LANES), f32),
            pltpu.VMEM((panels, panel, LANES), f32),
            dma((half + 1, 2)), dma((half + 1, 2)),
            dma((half + 1, rows)), dma((half + 1, rows)),
            dma((half + 1,)), dma((half + 1,)),
            dma((panels, tiles)), dma((panels, tiles)),
            dma((tiles,)), dma((tiles,)),
            dma((panels,)), dma((panels,)),
        ],
        compiler_params=pltpu.CompilerParams(
            vmem_limit_bytes=48 << 20, collective_id=0, has_side_effects=True
        ),
        cost_estimate=pl.CostEstimate(
            flops=6 * tall * wide * rows * width * half, bytes_accessed=2 * own.size * 2, transcendentals=0
        ),
    )(own, stiff.reshape(rows, 1, width), slot.reshape(rows, 1, width))


def zone_kernel(place_ref, source_ref, blocks_ref, scale_ref, out_ref):
    panels, tiles, panel, _ = blocks_ref.shape
    entries = source_ref.shape[1]
    me = place_ref[0]
    out_ref[...] = jnp.zeros_like(out_ref)
    scale = scale_ref[...]

    def one_tile(tile, carry):
        got = [blocks_ref[lax.rem(g - me + panels, panels), tile] for g in range(panels)]
        for k in range(entries):
            row = jnp.concatenate([b[:, k * panel : (k + 1) * panel] for b in got], axis=1)
            zone = source_ref[tile, k]
            out_ref[zone] += row * scale
        return carry

    lax.fori_loop(0, tiles, one_tile, 0)


def per_device(mode_shapes, stiffness, node_slot, slot_zone):
    panel = mode_shapes.shape[0]
    tiles = lax.axis_size("tile")
    panels = lax.axis_size("mode")
    modes = panel * panels
    entries = slot_zone.shape[2]
    owned = ZONES // tiles
    me = lax.axis_index("mode")
    tile = lax.axis_index("tile")

    own = mode_shapes.transpose(1, 0, 2)
    arrived, sums = pair_sums(own, stiffness, node_slot, tiles, panels, entries)
    totals = 0.5 * sums[:, :, 0].reshape(modes)
    source = lax.dynamic_index_in_dim(slot_zone, tile, 1, keepdims=False)
    mine = lax.dynamic_slice_in_dim(totals, me * panel, panel, 0)
    scale = (0.5 * ZONES) / jnp.sqrt(mine[:, None] * totals[None, :])
    return pl.pallas_call(
        zone_kernel,
        out_shape=jax.ShapeDtypeStruct((owned, panel, modes), jnp.float32),
        in_specs=[
            pl.BlockSpec(memory_space=pltpu.SMEM),
            pl.BlockSpec(memory_space=pltpu.SMEM),
            pl.BlockSpec(memory_space=pltpu.VMEM),
            pl.BlockSpec(memory_space=pltpu.VMEM),
        ],
        out_specs=pl.BlockSpec(memory_space=pltpu.VMEM),
    )(me.reshape(1), source, arrived, scale)


def solution(mesh):
    placed = (P("mode", "tile", None), P("tile", None), P("tile", None), P())
    return jax.shard_map(
        per_device, mesh=mesh, in_specs=placed, out_specs=P("tile", "mode", None), check_vma=False
    )
```

time: 126 us -> 53 us (0.42)
  the two profiles are of different devices: /device:TPU:0 before, /device:TPU:25 now
where the time goes in v2:
time: 53 us; the launch traced here: 52.8 us
  Pallas kernels  48.3 us (91%)
  local copies, waits for them, and re-layouts  3.69 us (7%)
  other arithmetic  0.77 us (1%)
    pallas_call x1, Pallas kernels, pair_sums(): pl.pallas_call(functools.partial(pair_kernel, (tiles, panels, entries)),...  45.4 us
    pallas_call x1, Pallas kernels, per_device(): pl.pallas_call(zone_kernel, out_shape=jax.ShapeDtypeStruct((owned, panel,...  2.84 us
    unnamed x9, local copies, waits for them, and re-layouts  2.83 us

profile of v2, /device:TPU:25, one launch (start us, length us, event | category | flops | bytes accessed | tf_op | source)
XLA Modules:
  0.0 52.8 jit_solution(7656036194929058570)
XLA Ops:
  0.0 0.0 copy-start
  0.0 0.0 copy-start.2
  0.0 1.4 %copy.11 = bf16[16,8,2048]{2,0,1:T(8,128)(2,1)S(1)} copy(bf16[16,8,2048]{2,1,0:T(8,128)(2,1)} %param.4) | data formatting | bytes 1048576 | tf_op args[0]
  1.4 0.0 copy-done.2
  1.4 0.0 copy-start.3
  1.5 0.8 %copy-done.3 = s32[8,2048]{1,0:T(8,128)S(1)} copy-done((s32[8,2048]{1,0:T(8,128)S(1)}, s32[8,2048]{1,0:T(8,128)}, u32[]{:S(2)}) %copy-start.3) | copy-done | bytes 65560
  2.3 45.4 %shard_map.46 = (f32[4,8,16,128]{3,2,1,0:T(8,128)S(1)}, f32[4,16,128]{2,1,0:T(8,128)S(1)}) custom-call(bf16[8,16,2048]{2,1,0:T(8,128)(2,1)S(1)} %bitcast.7, f32[8,1,2048]{2,1,0:T(1,128)S(1)} %reshape.18.stiff_ref, s32[8,1,2048]{2,1,0:T(1,128)S(1)} %reshape.19.slot_ref), custom_call_target="tpu_custom_call" | custom-call | flops 12884901888 | bytes 1048576 | tf_op jit(solution)/shard_map/pallas_call | solution.py:296
  47.7 0.0 copy-start.1
  47.7 0.7 %copy-done.1 = f32[4,8,16,128]{3,2,1,0:T(8,128)} copy-done((f32[4,8,16,128]{3,2,1,0:T(8,128)}, f32[4,8,16,128]{3,2,1,0:T(8,128)S(1)}, u32[]{:S(2)}) %copy-start.1) | copy-done | bytes 262168
  48.4 0.1 multiply_reduce_fusion
  48.5 0.1 mul.31
  48.6 0.1 dynamic_slice.8
  48.6 0.7 %rsqrt_multiply_fusion.scale_ref = f32[16,64]{1,0:T(8,128)} fusion(f32[64]{0:T(128)S(1)} %mul.31, f32[16]{0:T(128)S(1)} %dynamic_slice.8), kind=kLoop, calls=%fused_computation.2 | loop fusion | flops 2048 | bytes 4416 | tf_op jit(solution)/shard_map/div | solution.py:365
  49.3 0.0 copy-done
  49.3 0.6 %constant_dynamic-slice_fusion = s32[8,1,8]{2,1,0:T(1,128)} fusion(s32[8,8,8]{2,1,0:T(8,128)S(1)} %copy-done, s32[]{:T(128)S(6)} %select_n.7), kind=kLoop, calls=%fused_computation.3 | loop fusion | bytes 516 | tf_op jit(solution)/shard_map/jit(dynamic_index_in_dim)/dynamic_slice | solution.py:363
  49.9 2.8 %shard_map.47 = f32[64,16,64]{2,1,0:T(8,128)} custom-call(s32[1]{0:T(128)} %bitcast.place_ref, s32[8,8]{1,0:T(8,128)} %bitcast.8, f32[4,8,16,128]{3,2,1,0:T(8,128)} %copy-done.1, f32[16,64]{1,0:T(8,128)} %rsqrt_multiply_fusion.scale_ref), custom_call_target="tpu_custom_call" | custom-call | tf_op jit(solution)/shard_map/pallas_call | solution.py:366
  (2 shorter events, 0.1 us)
Async XLA Ops:
  0.0 49.3 %copy-start = (s32[8,8,8]{2,1,0:T(8,128)S(1)}, s32[8,8,8]{2,1,0:T(8,128)}, u32[]{:S(2)}) copy-start(s32[8,8,8]{2,1,0:T(8,128)} %param.7) | copy-start | bytes 6148
  0.0 1.4 %copy-start.2 = (f32[8,2048]{1,0:T(8,128)S(1)}, f32[8,2048]{1,0:T(8,128)}, u32[]{:S(2)}) copy-start(f32[8,2048]{1,0:T(8,128)} %param.5) | copy-start | bytes 196612
  1.4 0.8 %copy-start.3 = (s32[8,2048]{1,0:T(8,128)S(1)}, s32[8,2048]{1,0:T(8,128)}, u32[]{:S(2)}) copy-start(s32[8,2048]{1,0:T(8,128)} %param.6) | copy-start | bytes 196612
  47.7 0.7 %copy-start.1 = (f32[4,8,16,128]{3,2,1,0:T(8,128)}, f32[4,8,16,128]{3,2,1,0:T(8,128)S(1)}, u32[]{:S(2)}) copy-start(f32[4,8,16,128]{3,2,1,0:T(8,128)S(1)} %get-tuple-element.7.blocks_ref) | copy-start | bytes 786436

commit v3 on v2

--- a/solution.py
+++ b/solution.py
@@ -69,6 +69,14 @@
 
     lax.fori_loop(1, tiles, greet, 0)
 
+    def greet_far(step, carry):
+        pl.semaphore_signal(
+            barrier, inc=1, device_id=(tile_peer(step), mode_peer(half)), device_id_type=pl.DeviceIdType.MESH
+        )
+        return carry
+
+    lax.fori_loop(1, tiles, greet_far, 0)
+
     first_tile, last_tile = tile == 0, tile == tiles - 1
 
     @pl.when(first_tile)
@@ -83,7 +91,7 @@
             frames[d, rows + 1] = jnp.zeros((panel, width), jnp.bfloat16)
         half_frame[rows + 1] = jnp.zeros((panel, part), jnp.bfloat16)
 
-    pl.semaphore_wait(barrier, panels - 1 + tiles - 1)
+    pl.semaphore_wait(barrier, panels - 1 + 2 * (tiles - 1))
 
     their_start = pl.multiple_of(jnp.where(me < half, shift, 0), LANES)
     mine_start = pl.multiple_of(jnp.where(me < half, 0, shift), LANES)
@@ -150,6 +158,32 @@
     def back_copy(d):
         block = results.at[panels + d]
         return to(block, returned.at[d], back_send.at[d], back_recv.at[d], tile, mode_peer(d))
+
+    def far_copy(step):
+        peer = tile_peer(step)
+        return to(
+            results.at[panels + half, peer], arrived.at[panels, tile],
+            block_send.at[panels, step], block_recv.at[panels, step], peer, mode_peer(half),
+        )
+
+    def msum_copy(step):
+        return to(
+            mode_sums.at[me], mode_sums.at[me], msum_send.at[step], msum_recv.at[step], tile, mode_peer(step)
+        )
+
+    def pass_on():
+        def take_sum(step, carry):
+            tsum_copy(step).wait()
+            return carry
+
+        lax.fori_loop(1, tiles, take_sum, 0)
+        mode_sums[me] = jnp.sum(tile_sums[...], axis=0)
+        for step in range(1, panels):
+            msum_copy(step).start()
+        for e in range(1, half):
+            back_copy(e).wait()
+            results[panels - e] = returned[e]
+            start_blocks(panels - e)
 
     def tsum_copy(step):
         return to(sums, tile_sums.at[tile], tsum_send.at[step], tsum_recv.at[step], tile_peer(step), me)
@@ -182,6 +216,8 @@
                 if d == 1:
                     await_edges(0)
                 await_edges(d)
+                if split:
+                    pass_on()
 
             if split:
                 here = pl.ds(mine_start, part)
@@ -229,7 +265,17 @@
 
         lax.fori_loop(0, rows, one_row, 0)
         keep(panels + d, acc[pl.ds(tall, tall), pl.ds(0, wide)])
-        back_copy(d).start()
+        if split:
+
+            def send_far(step, carry):
+                far_copy(step).start()
+                return carry
+
+            lax.fori_loop(0, tiles, send_far, 0)
+        else:
+            back_copy(d).start()
+        keep(d, acc[pl.ds(0, tall), pl.ds(wide, wide)])
+        start_blocks(d)
         if d == 1:
 
             def send_sum(step, carry):
@@ -240,39 +286,14 @@
             tile_sums[tile] = sums[...]
             keep(0, acc[pl.ds(0, tall), pl.ds(0, wide)])
             start_blocks(0)
-        values = acc[pl.ds(0, tall), pl.ds(wide, wide)]
-        if split:
-            def take_sum(step, carry):
-                tsum_copy(step).wait()
-                return carry
-
-            lax.fori_loop(1, tiles, take_sum, 0)
-            mode_sums[me] = jnp.sum(tile_sums[...], axis=0)
-            msums = [
-                to(mode_sums.at[me], mode_sums.at[me], msum_send.at[step], msum_recv.at[step], tile, mode_peer(step))
-                for step in range(1, panels)
-            ]
-            for copy in msums:
-                copy.start()
-            for e in range(1, half):
-                back_copy(e).wait()
-                results[panels - e] = returned[e]
-                start_blocks(panels - e)
-            back_copy(d).wait()
-            keep(half, values)
-            results[half] += returned[half]
-            start_blocks(half)
-        else:
-            keep(d, values)
-            start_blocks(d)
 
     for d in range(half + 1):
         finish_edges(d)
     for d in range(1, half + 1):
         for row in range(rows):
             row_copy(d, row).wait_send()
-    for copy in msums:
-        copy.wait()
+    for step in range(1, panels):
+        msum_copy(step).wait()
 
     for block in range(panels):
         def take(step, carry):
@@ -280,7 +301,15 @@
             return carry
 
         lax.fori_loop(1, tiles, take, 0)
-    out_ref[...] = arrived[...]
+
+    def take_far(step, carry):
+        far_copy(step).wait()
+        return carry
+
+    lax.fori_loop(0, tiles, take_far, 0)
+    for block in range(panels):
+        out_ref[block] = arrived[block]
+    out_ref[half] += arrived[panels]
     total_ref[...] = mode_sums[...]
 
 
@@ -309,14 +338,14 @@
             pltpu.VMEM((tall, wide), f32),
             pltpu.VMEM((panel, LANES), f32),
             pltpu.VMEM((panels + half + 1,) + blocks[1:], f32),
-            pltpu.VMEM((half + 1,) + blocks[1:], f32),
-            pltpu.VMEM(blocks, f32),
+            pltpu.VMEM((half,) + blocks[1:], f32),
+            pltpu.VMEM((panels + 1,) + blocks[1:], f32),
             pltpu.VMEM((tiles, panel, LANES), f32),
             pltpu.VMEM((panels, panel, LANES), f32),
             dma((half + 1, 2)), dma((half + 1, 2)),
             dma((half + 1, rows)), dma((half + 1, rows)),
-            dma((half + 1,)), dma((half + 1,)),
-            dma((panels, tiles)), dma((panels, tiles)),
+            dma((half,)), dma((half,)),
+            dma((panels + 1, tiles)), dma((panels + 1, tiles)),
             dma((tiles,)), dma((tiles,)),
             dma((panels,)), dma((panels,)),
         ],
@@ -329,18 +358,27 @@
     )(own, stiff.reshape(rows, 1, width), slot.reshape(rows, 1, width))
 
 
-def zone_kernel(place_ref, source_ref, blocks_ref, scale_ref, out_ref):
+def zone_kernel(place_ref, source_ref, blocks_ref, sums_ref, out_ref):
     panels, tiles, panel, _ = blocks_ref.shape
-    entries = source_ref.shape[1]
-    me = place_ref[0]
+    entries = source_ref.shape[2]
+    tile, me = place_ref[0], place_ref[1]
     out_ref[...] = jnp.zeros_like(out_ref)
-    scale = scale_ref[...]
-
-    def one_tile(tile, carry):
-        got = [blocks_ref[lax.rem(g - me + panels, panels), tile] for g in range(panels)]
+    shape = (panel, panel)
+    diagonal = lax.broadcasted_iota(jnp.int32, shape, 0) == lax.broadcasted_iota(jnp.int32, shape, 1)
+    across = jnp.concatenate(
+        [
+            jnp.sum(jnp.where(diagonal, sums_ref[g][:, :panel], 0.0), axis=0, keepdims=True)
+            for g in range(panels)
+        ],
+        axis=1,
+    )
+    scale = (0.5 * ZONES) / jnp.sqrt((0.5 * sums_ref[me][:, :1]) * (0.5 * across))
+
+    def one_tile(source, carry):
+        got = [blocks_ref[lax.rem(g - me + panels, panels), source] for g in range(panels)]
         for k in range(entries):
             row = jnp.concatenate([b[:, k * panel : (k + 1) * panel] for b in got], axis=1)
-            zone = source_ref[tile, k]
+            zone = source_ref[source, tile, k]
             out_ref[zone] += row * scale
         return carry
 
@@ -354,15 +392,10 @@
     modes = panel * panels
     entries = slot_zone.shape[2]
     owned = ZONES // tiles
-    me = lax.axis_index("mode")
-    tile = lax.axis_index("tile")
+    place = jnp.stack([lax.axis_index("tile"), lax.axis_index("mode")]).astype(jnp.int32)
 
     own = mode_shapes.transpose(1, 0, 2)
     arrived, sums = pair_sums(own, stiffness, node_slot, tiles, panels, entries)
-    totals = 0.5 * sums[:, :, 0].reshape(modes)
-    source = lax.dynamic_index_in_dim(slot_zone, tile, 1, keepdims=False)
-    mine = lax.dynamic_slice_in_dim(totals, me * panel, panel, 0)
-    scale = (0.5 * ZONES) / jnp.sqrt(mine[:, None] * totals[None, :])
     return pl.pallas_call(
         zone_kernel,
         out_shape=jax.ShapeDtypeStruct((owned, panel, modes), jnp.float32),
@@ -373,7 +406,7 @@
             pl.BlockSpec(memory_space=pltpu.VMEM),
         ],
         out_specs=pl.BlockSpec(memory_space=pltpu.VMEM),
-    )(me.reshape(1), source, arrived, scale)
+    )(place, slot_zone, arrived, sums)
 
 
 def solution(mesh):

time: 53 us -> 51.4 us (0.970)
  the two profiles are of different devices: /device:TPU:25 before, /device:TPU:0 now
where the time goes in v3:
time: 51.4 us; the launch traced here: 51.2 us
  Pallas kernels  47 us (91%)
  local copies, waits for them, and re-layouts  3.6 us (7%)
  other arithmetic  0.6 us (1%)
    pallas_call x1, Pallas kernels, pair_sums(): pl.pallas_call(functools.partial(pair_kernel, (tiles, panels, entries)),...  43.8 us
    pallas_call x1, Pallas kernels, per_device(): pl.pallas_call(zone_kernel, out_shape=jax.ShapeDtypeStruct((owned, panel,...  3.15 us
    unnamed x7, local copies, waits for them, and re-layouts  2.63 us

profile of v3, /device:TPU:0, one launch (start us, length us, event | category | flops | bytes accessed | tf_op | source)
XLA Modules:
  0.0 51.2 jit_solution(822404961486374163)
XLA Ops:
  0.0 0.6 %pad_add_fusion.place_ref = s32[2]{0:T(128)} fusion(s32[1]{0:T(128)} %bitcast.1, s32[1]{0:T(128)} %bitcast), kind=kLoop, calls=%fused_computation.1 | loop fusion | flops 2 | bytes 16 | tf_op jit(solution)/shard_map/stack | solution.py:395
  0.6 0.0 copy-start.2
  0.6 0.9 %reshape.6.stiff_ref = f32[8,1,2048]{2,1,0:T(1,128)S(1)} reshape(f32[8,2048]{1,0:T(8,128)} %param.5) | data formatting | bytes 131072 | tf_op jit(solution)/shard_map/reshape | solution.py:358
  1.5 0.0 copy-done.2
  1.6 1.3 %copy.7 = bf16[16,8,2048]{2,0,1:T(8,128)(2,1)S(1)} copy(bf16[16,8,2048]{2,1,0:T(8,128)(2,1)} %param.4) | data formatting | bytes 1048576 | tf_op args[0]
  2.9 43.8 %shard_map.46 = (f32[4,8,16,128]{3,2,1,0:T(8,128)S(1)}, f32[4,16,128]{2,1,0:T(8,128)S(1)}) custom-call(bf16[8,16,2048]{2,1,0:T(8,128)(2,1)S(1)} %bitcast.5, f32[8,1,2048]{2,1,0:T(1,128)S(1)} %reshape.6.stiff_ref, s32[8,1,2048]{2,1,0:T(1,128)S(1)} %reshape.7.slot_ref), custom_call_target="tpu_custom_call" | custom-call | flops 12884901888 | bytes 1048576 | tf_op jit(solution)/shard_map/pallas_call | solution.py:325
  46.8 0.0 copy-start
  46.8 0.7 %copy-done = f32[4,8,16,128]{3,2,1,0:T(8,128)} copy-done((f32[4,8,16,128]{3,2,1,0:T(8,128)}, f32[4,8,16,128]{3,2,1,0:T(8,128)S(1)}, u32[]{:S(2)}) %copy-start) | copy-done | bytes 262168
  47.4 0.0 copy-start.1
  47.4 0.6 %copy-done.1 = f32[4,16,128]{2,1,0:T(8,128)} copy-done((f32[4,16,128]{2,1,0:T(8,128)}, f32[4,16,128]{2,1,0:T(8,128)S(1)}, u32[]{:S(2)}) %copy-start.1) | copy-done | bytes 32792
  48.1 3.1 %shard_map.47 = f32[64,16,64]{2,1,0:T(8,128)} custom-call(s32[2]{0:T(128)} %pad_add_fusion.place_ref, s32[8,8,8]{2,1,0:T(8,128)} %source_ref.1, f32[4,8,16,128]{3,2,1,0:T(8,128)} %copy-done, f32[4,16,128]{2,1,0:T(8,128)} %copy-done.1), custom_call_target="tpu_custom_call" | custom-call | tf_op jit(solution)/shard_map/pallas_call | solution.py:399
  (1 shorter events, 0.0 us)
Async XLA Ops:
  0.6 0.9 %copy-start.2 = (s32[8,2048]{1,0:T(8,128)S(1)}, s32[8,2048]{1,0:T(8,128)}, u32[]{:S(2)}) copy-start(s32[8,2048]{1,0:T(8,128)} %param.6) | copy-start | bytes 196612
  46.8 0.7 %copy-start = (f32[4,8,16,128]{3,2,1,0:T(8,128)}, f32[4,8,16,128]{3,2,1,0:T(8,128)S(1)}, u32[]{:S(2)}) copy-start(f32[4,8,16,128]{3,2,1,0:T(8,128)S(1)} %get-tuple-element.7.blocks_ref) | copy-start | bytes 786436
  47.4 0.6 %copy-start.1 = (f32[4,16,128]{2,1,0:T(8,128)}, f32[4,16,128]{2,1,0:T(8,128)S(1)}, u32[]{:S(2)}) copy-start(f32[4,16,128]{2,1,0:T(8,128)S(1)} %get-tuple-element.8.sums_ref) | copy-start | bytes 98308

commit v4 on v3

--- a/solution.py
+++ b/solution.py
@@ -130,10 +130,7 @@
 
     start_edges(0)
     for d in range(1, half + 1):
-        row_copy(d, 0).start()
-        row_copy(d, rows - 1).start()
-    for d in range(1, half + 1):
-        for row in range(1, rows - 1):
+        for row in (0, rows - 1, *range(1, rows - 1)):
             row_copy(d, row).start()
     for row in range(rows):
         frames[0, row + 1] = own_ref[row]
@@ -358,10 +355,10 @@
     )(own, stiff.reshape(rows, 1, width), slot.reshape(rows, 1, width))
 
 
-def zone_kernel(place_ref, source_ref, blocks_ref, sums_ref, out_ref):
+def zone_kernel(source_ref, blocks_ref, sums_ref, out_ref):
     panels, tiles, panel, _ = blocks_ref.shape
     entries = source_ref.shape[2]
-    tile, me = place_ref[0], place_ref[1]
+    tile, me = lax.axis_index("tile"), lax.axis_index("mode")
     out_ref[...] = jnp.zeros_like(out_ref)
     shape = (panel, panel)
     diagonal = lax.broadcasted_iota(jnp.int32, shape, 0) == lax.broadcasted_iota(jnp.int32, shape, 1)
@@ -392,7 +389,6 @@
     modes = panel * panels
     entries = slot_zone.shape[2]
     owned = ZONES // tiles
-    place = jnp.stack([lax.axis_index("tile"), lax.axis_index("mode")]).astype(jnp.int32)
 
     own = mode_shapes.transpose(1, 0, 2)
     arrived, sums = pair_sums(own, stiffness, node_slot, tiles, panels, entries)
@@ -401,12 +397,11 @@
         out_shape=jax.ShapeDtypeStruct((owned, panel, modes), jnp.float32),
         in_specs=[
             pl.BlockSpec(memory_space=pltpu.SMEM),
-            pl.BlockSpec(memory_space=pltpu.SMEM),
             pl.BlockSpec(memory_space=pltpu.VMEM),
             pl.BlockSpec(memory_space=pltpu.VMEM),
         ],
         out_specs=pl.BlockSpec(memory_space=pltpu.VMEM),
-    )(place, slot_zone, arrived, sums)
+    )(slot_zone, arrived, sums)
 
 
 def solution(mesh):

time: 51.4 us -> 49.8 us (0.969)
  Pallas kernels: 47 us -> 46 us
  other arithmetic: 0.6 us -> 0 us
    pallas_call x1, Pallas kernels: 43.8 us -> 42.8 us  [pair_sums(): pl.pallas_call(functools.partial(pair_kernel, (tiles, panels, entries)),...]
    another operation x1 -> x0, other arithmetic: 0.6 us -> none  [per_device(): jnp.stack([lax.axis_index('tile'), lax.axis_index('mode')])]
where the time goes in v4:
time: 49.8 us; the launch traced here: 49.6 us
  Pallas kernels  46 us (92%)
  local copies, waits for them, and re-layouts  3.6 us (7%)
    pallas_call x1, Pallas kernels, pair_sums(): pl.pallas_call(functools.partial(pair_kernel, (tiles, panels, entries)),...  42.8 us
    pallas_call x1, Pallas kernels, per_device(): pl.pallas_call(zone_kernel, out_shape=jax.ShapeDtypeStruct((owned, panel,...  3.13 us
    unnamed x7, local copies, waits for them, and re-layouts  2.63 us

profile of v4, /device:TPU:0, one launch (start us, length us, event | category | flops | bytes accessed | tf_op | source)
XLA Modules:
  0.0 49.6 jit_solution(11219590073123607249)
XLA Ops:
  0.0 0.0 copy-start.2
  0.0 0.9 %reshape.6.stiff_ref = f32[8,1,2048]{2,1,0:T(1,128)S(1)} reshape(f32[8,2048]{1,0:T(8,128)} %param.5) | data formatting | bytes 131072 | tf_op jit(solution)/shard_map/reshape | solution.py:355
  0.9 0.0 copy-done.2
  1.0 1.3 %copy.7 = bf16[16,8,2048]{2,0,1:T(8,128)(2,1)S(1)} copy(bf16[16,8,2048]{2,1,0:T(8,128)(2,1)} %param.4) | data formatting | bytes 1048576 | tf_op args[0]
  2.3 42.8 %shard_map.46 = (f32[4,8,16,128]{3,2,1,0:T(8,128)S(1)}, f32[4,16,128]{2,1,0:T(8,128)S(1)}) custom-call(bf16[8,16,2048]{2,1,0:T(8,128)(2,1)S(1)} %bitcast.3, f32[8,1,2048]{2,1,0:T(1,128)S(1)} %reshape.6.stiff_ref, s32[8,1,2048]{2,1,0:T(1,128)S(1)} %reshape.7.slot_ref), custom_call_target="tpu_custom_call" | custom-call | flops 12884901888 | bytes 1048576 | tf_op jit(solution)/shard_map/pallas_call | solution.py:322
  45.2 0.0 copy-start
  45.2 0.7 %copy-done = f32[4,8,16,128]{3,2,1,0:T(8,128)} copy-done((f32[4,8,16,128]{3,2,1,0:T(8,128)}, f32[4,8,16,128]{3,2,1,0:T(8,128)S(1)}, u32[]{:S(2)}) %copy-start) | copy-done | bytes 262168
  45.9 0.0 copy-start.1
  45.9 0.6 %copy-done.1 = f32[4,16,128]{2,1,0:T(8,128)} copy-done((f32[4,16,128]{2,1,0:T(8,128)}, f32[4,16,128]{2,1,0:T(8,128)S(1)}, u32[]{:S(2)}) %copy-start.1) | copy-done | bytes 32792
  46.5 3.1 %shard_map.47 = f32[64,16,64]{2,1,0:T(8,128)} custom-call(s32[8,8,8]{2,1,0:T(8,128)} %source_ref.1, f32[4,8,16,128]{3,2,1,0:T(8,128)} %copy-done, f32[4,16,128]{2,1,0:T(8,128)} %copy-done.1), custom_call_target="tpu_custom_call" | custom-call | tf_op jit(solution)/shard_map/pallas_call | solution.py:395
  (1 shorter events, 0.0 us)
Async XLA Ops:
  0.0 0.9 %copy-start.2 = (s32[8,2048]{1,0:T(8,128)S(1)}, s32[8,2048]{1,0:T(8,128)}, u32[]{:S(2)}) copy-start(s32[8,2048]{1,0:T(8,128)} %param.6) | copy-start | bytes 196612
  45.2 0.7 %copy-start = (f32[4,8,16,128]{3,2,1,0:T(8,128)}, f32[4,8,16,128]{3,2,1,0:T(8,128)S(1)}, u32[]{:S(2)}) copy-start(f32[4,8,16,128]{3,2,1,0:T(8,128)S(1)} %get-tuple-element.7.blocks_ref) | copy-start | bytes 786436
  45.9 0.6 %copy-start.1 = (f32[4,16,128]{2,1,0:T(8,128)}, f32[4,16,128]{2,1,0:T(8,128)S(1)}, u32[]{:S(2)}) copy-start(f32[4,16,128]{2,1,0:T(8,128)S(1)} %get-tuple-element.8.sums_ref) | copy-start | bytes 98308
